TPU v7x, 256 devices: a whole 4x4x8 slice. The times are simulated.
256 devices in a mesh: row: 32 (over x_hi, z, core), cent: 8 (over y, x_lo).
Axes of the slice: x: 4 (x_hi: 2, x_lo: 2; x = x_hi * 2 + x_lo), y: 4, z: 8, core: 2. Of those that a mesh axis runs over, the one named last changes fastest.
Arguments:
- embedding_pool: bfloat16 [262144, 512], P('row')
- select_index: int32 [131072], P('row'), may hold values from 0 to 8191
- seed_index: int32 [4096], P('cent'), may hold values from 0 to 131071
Outputs:
- centroids: bfloat16 [4096, 512], P('cent')
- row_energy: float32 [131072], P('row')
All inputs are finite; a program needn't handle non-finite values.
Results may differ from a plain program's by a relative error of at most 0.0036.
Values may be sent and summed in bfloat16 or wider, within the bound.
A program may use at most 64 MiB of HBM per device.

v0:
```python
import jax
import jax.numpy as jnp
from jax import lax
from jax.sharding import PartitionSpec as P

ITERS = 2


def normalize(vectors):
    return vectors * lax.rsqrt(jnp.sum(vectors * vectors, axis=1, keepdims=True) + 1e-06)


def on_device(embedding_pool, select_index, seed_index):
    sample = jnp.take(embedding_pool, select_index, axis=0)
    row_count = sample.shape[0]
    first_row = lax.axis_index("row") * row_count
    positions = first_row + jnp.arange(row_count, dtype=jnp.int32)
    picker = (seed_index[:, None] == positions[None, :]).astype(jnp.bfloat16)
    seeded = lax.psum(
        jnp.dot(picker, sample, preferred_element_type=jnp.float32).astype(jnp.bfloat16), "row"
    ).astype(jnp.float32)
    centers = normalize(seeded).astype(jnp.bfloat16)
    energy = jnp.zeros((row_count,), jnp.float32)
    for iteration in range(ITERS):
        scores = lax.dot_general(
            sample, centers, (((1,), (1,)), ((), ())), preferred_element_type=jnp.float32
        )
        local_top = jnp.max(scores, axis=1)
        top = lax.pmax(local_top, "cent")
        expo = jnp.exp(scores - top[:, None])
        total = lax.psum(jnp.sum(expo, axis=1), "cent")
        weights = expo / total[:, None]
        probs = weights.astype(jnp.bfloat16)
        sums = lax.dot_general(
            probs, sample, (((0,), (0,)), ((), ())), preferred_element_type=jnp.float32
        )
        sums = lax.psum(sums, "row")
        centers = normalize(sums).astype(jnp.bfloat16)
        energy = top + jnp.log(total)
    return (centers, energy)


def solution(mesh):
    placed = (P("row", None), P("row"), P("cent"))
    return jax.shard_map(
        on_device,
        mesh=mesh,
        in_specs=placed,
        out_specs=(P("cent", None), P("row")),
        check_vma=False,
    )
```

profile of v0, /device:TPU:1, one launch (start us, length us, event | category | flops | bytes accessed | tf_op | source)
XLA Modules:
  0.0 1006.2 jit_solution(9333915565382986733)
XLA Ops:
  7.2 0.0 all-reduce.4.cloned.1.call-start
  7.2 0.7 compare_and_fusion
  7.9 0.7 fusion.18
  8.7 0.0 copy-start
  8.7 21.9 %gather_fusion = bf16[4096,512]{1,0:T(8,128)(2,1)} fusion(bf16[8192,512]{1,0:T(8,128)(2,1)} %param.3, s32[4096]{0:T(1024)S(1)} %fusion.18), kind=kCustom, calls=%fused_computation | custom fusion | bytes 8404992 | tf_op jit(solution)/shard_map/jit(_take)/gather | solution.py:14
  30.6 0.0 copy-done
  30.6 5.4 fusion.8
  36.0 0.0 all-reduce.4.cloned.1.call-update
  36.0 0.0 all-reduce.6.cloned.1.call-start
  36.0 269.9 %all-reduce.4.cloned.1.call-done = bf16[512,512]{1,0:T(8,128)(2,1)} async-done(((bf16[512,512]{1,0:T(8,128)(2,1)}), bf16[512,512]{1,0:T(8,128)(2,1)}) %all-reduce.4.cloned.1.call-update) | async-done | bytes 524304 | tf_op jit(solution)/shard_map/psum | solution.py:19
  305.9 1.2 fusion.11
  307.1 6.5 fusion.19
  313.6 26.3 %pmax.14 = f32[4096]{0:T(1024)S(1)} all-reduce(f32[4096]{0:T(1024)S(1)} %get-tuple-element.2), channel_id=1, replica_groups=mesh['row'=32,'cent'=8] {'cent'}, use_global_device_ids=true, to_apply=%region_3.4 | all-reduce | flops 4096 | bytes 32768 | tf_op jit(solution)/shard_map/pmax | solution.py:29
  340.0 4.5 fusion.2
  344.5 23.8 %psum.36 = f32[4096]{0:T(1024)S(1)} all-reduce(f32[4096]{0:T(1024)S(1)} %fusion.2), channel_id=1, replica_groups=mesh['row'=32,'cent'=8] {'cent'}, use_global_device_ids=true, to_apply=%region_5.6 | all-reduce | flops 4096 | bytes 32768 | tf_op jit(solution)/shard_map/psum | solution.py:31
  368.3 7.0 fusion.6
  375.3 0.0 all-reduce.6.cloned.1.call-update
  375.3 0.0 all-reduce.8.cloned.1.call-start
  375.4 275.2 %all-reduce.6.cloned.1.call-done = f32[512,512]{1,0:T(8,128)} async-done(((f32[512,512]{1,0:T(8,128)}), f32[512,512]{1,0:T(8,128)}) %all-reduce.6.cloned.1.call-update) | async-done | bytes 1048592 | tf_op jit(solution)/shard_map/psum | solution.py:37
  650.6 1.4 multiply_reduce_fusion.1
  652.0 6.7 fusion.20
  658.7 26.3 %pmax.15 = f32[4096]{0:T(1024)S(1)} all-reduce(f32[4096]{0:T(1024)S(1)} %get-tuple-element.4), channel_id=1, replica_groups=mesh['row'=32,'cent'=8] {'cent'}, use_global_device_ids=true, to_apply=%region_9.10 | all-reduce | flops 4096 | bytes 32768 | tf_op jit(solution)/shard_map/pmax | solution.py:29
  685.0 4.5 fusion.3
  689.5 23.8 %psum.38 = f32[4096]{0:T(1024)S(1)} all-reduce(f32[4096]{0:T(1024)S(1)} %fusion.3), channel_id=1, replica_groups=mesh['row'=32,'cent'=8] {'cent'}, use_global_device_ids=true, to_apply=%region_11.12 | all-reduce | flops 4096 | bytes 32768 | tf_op jit(solution)/shard_map/psum | solution.py:31
  713.3 7.1 fusion.7
  720.4 0.0 all-reduce.8.cloned.1.call-update
  720.4 0.6 log_add_fusion
  721.0 275.0 %all-reduce.8.cloned.1.call-done = f32[512,512]{1,0:T(8,128)} async-done(((f32[512,512]{1,0:T(8,128)}), f32[512,512]{1,0:T(8,128)}) %all-reduce.8.cloned.1.call-update) | async-done | bytes 1048592 | tf_op jit(solution)/shard_map/psum | solution.py:37
  996.1 1.4 multiply_reduce_fusion
  997.5 2.2 multiply_convert_fusion
  (4 shorter events, 0.0 us)
Async XLA Ops:
  7.2 298.7 %all-reduce.4.cloned.1.call-start = ((), (), s32[]{:S(2)}) async-start(), calls=%async_computation | async-start | bytes 1048576 | tf_op jit(solution)/shard_map/psum | solution.py:19
  8.7 21.9 %copy-start = (s32[512]{0:T(512)S(1)}, s32[512]{0:T(512)}, u32[]{:S(2)}) copy-start(s32[512]{0:T(512)} %param.5) | copy-start | bytes 6148
  36.0 614.6 %all-reduce.6.cloned.1.call-start = ((), (), s32[]{:S(2)}) async-start(), calls=%async_computation.1 | async-start | bytes 2097152 | tf_op jit(solution)/shard_map/psum | solution.py:37
  375.3 620.7 %all-reduce.8.cloned.1.call-start = ((), (), s32[]{:S(2)}) async-start(), calls=%async_computation.2 | async-start | bytes 2097152 | tf_op jit(solution)/shard_map/psum | solution.py:37
Sparse Core Ops, SparseCore 0:
  36.1 269.7 all-reduce.3
  375.5 275.0 all-reduce.5
  720.5 275.4 all-reduce.7
where the time goes:
time: 1010 us
  waiting for transfers between devices  820 us (81%)
  blocking collectives  100 us (10%)
  matrix products  32.6 us (3%)
  local copies, waits for them, and re-layouts  21.9 us (2%)
  other arithmetic  17.3 us (2%)
  between operations  13.8 us (1%)
    psum x2, waiting for transfers between devices, on_device(): sums = lax.psum(sums, 'row')  550 us
    psum x1, waiting for transfers between devices, on_device(): lax.psum(jnp.dot(picker, sample, preferred_element_type=jnp.float32).asty...  270 us
    pmax x2, blocking collectives, on_device(): top = lax.pmax(local_top, 'cent')  52.6 us
    psum x2, blocking collectives, on_device(): total = lax.psum(jnp.sum(expo, axis=1), 'cent')  47.7 us
    gather x1, local copies, waits for them, and re-layouts, on_device(): sample = jnp.take(embedding_pool, select_index, axis=0)  21.9 us
  transfers between devices with their start and end apart: 3, of which 3 were waited for; matrix products, arithmetic and copies ran while one was open for 0% of the time, Pallas kernels for 0%

commit v1 on v0

v1 whole, which is shorter than its diff:
```python
import jax
import jax.numpy as jnp
from jax import lax
from jax.experimental import pallas as pl
from jax.experimental.pallas import tpu as pltpu
from jax.sharding import PartitionSpec as P

F32 = jnp.float32
BF16 = jnp.bfloat16
MESH = pl.DeviceIdType.MESH

POOL = 8192
ROWS = 4096
CENT = 512
D = 512
LANES = 128
PARTS = D // LANES
LOADS = 8
BLOCK = 512
BLOCKS = ROWS // BLOCK
GROUPS = 4
GROUP = ROWS // GROUPS
OWN = 16
Z = 8
CENTS = 8
FAR_FIRST = (4, 3, 5, 2, 6, 1, 7)


def rows(start, size):
    return pl.ds(pl.multiple_of(start, size), size)


def kernel(
    pool_hbm,
    select,
    seed,
    centers_out,
    energy_out,
    pool_in,
    pool32,
    sample32,
    sample,
    seeds32,
    expo,
    scores,
    stats,
    scale,
    sums,
    seeds16,
    core16,
    x16,
    xs16,
    z16,
    zs16,
    own32,
    core32,
    x32,
    xs32,
    z32,
    zs32,
    centers,
    load_sem,
    rs_send,
    rs_recv,
    ag_send,
    ag_recv,
    stat_send,
    stat_recv,
):
    row = lax.axis_index("row")
    cent = lax.axis_index("cent")
    xh = row // 16
    z = (row // 2) % Z
    core = row % 2

    def row_id(xh_, z_, core_):
        return xh_ * 16 + z_ * 2 + core_

    sibling = (row_id(xh, z, 1 - core), cent)
    across = (row_id(1 - xh, z, core), cent)

    def z_id(distance):
        return (row_id(xh, (z + distance) % Z, core), cent)

    def cent_id(distance):
        return (row, (cent + distance) % CENTS)

    sent = []

    def send(src, dst, send_sem, recv_sem, device):
        copy = pltpu.make_async_remote_copy(
            src_ref=src, dst_ref=dst, send_sem=send_sem, recv_sem=recv_sem,
            device_id=device, device_id_type=MESH,
        )
        copy.start()
        sent.append(copy)

    def arrived(dst, send_sem, recv_sem, device):
        pltpu.make_async_remote_copy(
            src_ref=dst, dst_ref=dst, send_sem=send_sem, recv_sem=recv_sem,
            device_id=device, device_id_type=MESH,
        ).wait_recv()

    step = POOL // LOADS
    loads = []
    for i in range(LOADS):
        part = pl.ds(i * step, step)
        copy = pltpu.make_async_copy(pool_hbm.at[part], pool_in.at[part], load_sem.at[i])
        copy.start()
        loads.append(copy)
    barrier = pltpu.get_barrier_semaphore()
    partners = [sibling, across] + [z_id(d) for d in range(1, Z)] + [cent_id(d) for d in range(1, CENTS)]
    for partner in partners:
        pl.semaphore_signal(barrier, inc=1, device_id=partner, device_id_type=MESH)

    for i in range(LOADS):
        loads[i].wait()

        def widen(b, carry, i=i):
            start = i * step + b * 32
            block = pool_in[rows(start, 32), :].astype(F32)
            for t in range(PARTS):
                pool32[pl.ds(start * PARTS + t, 32, stride=PARTS), :] = block[:, t * LANES : (t + 1) * LANES]
            return carry

        lax.fori_loop(0, step // 32, widen, 0)

    pool32[POOL * PARTS :, :] = jnp.zeros((2 * PARTS, LANES), F32)

    def pick_seed(b, carry):
        for u in range(8):
            k = b * 8 + u
            where = seed[k]
            away = lax.shift_right_arithmetic(where, 12) - row
            away = jnp.minimum(jnp.maximum(away, -away), 1)
            index = select[jnp.bitwise_and(where, ROWS - 1)]
            index = index + (POOL - index) * away
            seeds32[pl.ds(pl.multiple_of(k * PARTS, PARTS), PARTS), :] = pool32[pl.ds(index * PARTS, PARTS), :]
        return carry

    lax.fori_loop(0, CENT // 8, pick_seed, 0)
    seeds16[...] = seeds32[...].astype(BF16)

    pl.semaphore_wait(barrier, len(partners))

    def reduce_scatter(phase, u, src, core_rx, x_rx, x_tx, z_rx, z_tx):
        dtype = src.dtype
        half = Z * u
        arrived(core_rx, rs_send.at[phase, 0], rs_recv.at[phase, 0], sibling)
        for d in FAR_FIRST + (0,):
            w = (z + d) % Z
            theirs = (1 - xh) * half + w * u
            x_tx[d] = (src[rows(core * 2 * half + theirs, u), :].astype(F32)
                       + core_rx[rows(theirs, u), :].astype(F32)).astype(dtype)
            send(x_tx.at[d], x_rx.at[d], rs_send.at[phase, 1 + d], rs_recv.at[phase, 1 + d], across)
        for d in FAR_FIRST + (0,):
            w = (z + d) % Z
            mine = xh * half + w * u
            arrived(x_rx.at[d], rs_send.at[phase, 1 + d], rs_recv.at[phase, 1 + d], across)
            total = (src[rows(core * 2 * half + mine, u), :].astype(F32)
                     + core_rx[rows(mine, u), :].astype(F32)) + x_rx[d].astype(F32)
            if d:
                z_tx[d] = total.astype(dtype)
                send(z_tx.at[d], z_rx.at[d], rs_send.at[phase, 8 + d], rs_recv.at[phase, 8 + d], z_id(d))
        for d in range(1, Z):
            arrived(z_rx.at[d], rs_send.at[phase, 8 + d], rs_recv.at[phase, 8 + d], z_id(Z - d))
            total = total + z_rx[d].astype(F32)
        return total

    def normalize(v):
        return v * lax.rsqrt(jnp.sum(v * v, axis=1, keepdims=True) + 1e-06)

    def all_gather(phase, dst):
        def part(xh_, z_, core_):
            return dst.at[rows(core_ * 256 + xh_ * 128 + z_ * OWN, OWN)]

        def sems(i):
            return ag_send.at[phase, i], ag_recv.at[phase, i]

        mine = part(xh, z, core)
        for d in FAR_FIRST:
            send(mine, mine, *sems(d), z_id(d))
        send(mine, mine, *sems(8), across)
        send(mine, mine, *sems(16), sibling)
        near_first = FAR_FIRST[::-1]
        for d in near_first:
            block = part(xh, (z - d + Z) % Z, core)
            arrived(block, *sems(d), z_id(Z - d))
            send(block, block, *sems(8 + d), across)
            send(block, block, *sems(16 + d), sibling)
        for d in (0,) + near_first:
            block = part(1 - xh, (z - d + Z) % Z, core)
            arrived(block, *sems(8 + d), across)
            send(block, block, *sems(24 + d), sibling)
        for d in (0,) + near_first:
            arrived(part(xh, (z - d + Z) % Z, 1 - core), *sems(16 + d), sibling)
            arrived(part(1 - xh, (z - d + Z) % Z, 1 - core), *sems(24 + d), sibling)

    u = OWN * PARTS
    send(
        seeds16.at[rows((1 - core) * 16 * u, 16 * u)], core16,
        rs_send.at[0, 0], rs_recv.at[0, 0], sibling,
    )

    def gather(b, carry):
        for v in range(16):
            i = b * 16 + v
            index = select[i]
            sample32[pl.ds(pl.multiple_of(i * PARTS, PARTS), PARTS), :] = pool32[
                pl.ds(index * PARTS, PARTS), :
            ]
        return carry

    lax.fori_loop(0, ROWS // 16, gather, 0)

    def narrow(b, carry):
        start = b * 32
        for t in range(PARTS):
            sample[rows(start, 32), t * LANES : (t + 1) * LANES] = sample32[
                pl.ds(start * PARTS + t, 32, stride=PARTS), :
            ].astype(BF16)
        return carry

    lax.fori_loop(0, ROWS // 32, narrow, 0)

    own32[...] = reduce_scatter(0, u, seeds16, core16, x16, xs16, z16, zs16)
    seeded = jnp.concatenate([own32[pl.ds(t, OWN, stride=PARTS), :] for t in range(PARTS)], axis=1)
    mine = rows(core * 256 + xh * 128 + z * OWN, OWN)
    centers[0, mine, :] = normalize(seeded).astype(BF16)
    all_gather(0, centers.at[0])

    for it in range(2):
        current = centers.at[it]

        def score(j, slot):
            scores[slot] = lax.dot_general(
                current[...], sample[rows(j * BLOCK, BLOCK), :],
                (((1,), (1,)), ((), ())), preferred_element_type=F32,
            )

        def soften(j, slot):
            top = [scores[slot, 8 * i : 8 * i + 8, :] for i in range(2)]
            for i in range(2, CENT // 8):
                top[i % 2] = jnp.maximum(top[i % 2], scores[slot, 8 * i : 8 * i + 8, :])
            top = jnp.max(jnp.maximum(top[0], top[1]), axis=0, keepdims=True)
            total = [jnp.zeros((8, BLOCK), F32)] * 2
            for i in range(CENT // 8):
                e = jnp.exp(scores[slot, 8 * i : 8 * i + 8, :] - top)
                expo[j, 8 * i : 8 * i + 8, :] = e
                total[i % 2] = total[i % 2] + e
            total = jnp.sum(total[0] + total[1], axis=0, keepdims=True)
            g = j // (BLOCKS // GROUPS)
            columns = rows((j % (BLOCKS // GROUPS)) * BLOCK, BLOCK)
            stats[it, g, 0, 0:1, columns] = top
            stats[it, g, 0, 1:2, columns] = total

        score(0, 0)
        for g in range(GROUPS):
            for j in range(g * BLOCKS // GROUPS, (g + 1) * BLOCKS // GROUPS):
                if j + 1 < BLOCKS:
                    score(j + 1, (j + 1) % 2)
                soften(j, j % 2)
            for d in range(1, CENTS):
                send(
                    stats.at[it, g, 0], stats.at[it, g, d],
                    stat_send.at[it, g, d], stat_recv.at[it, g, d], cent_id(d),
                )

        def merge(g):
            for d in range(1, CENTS):
                arrived(
                    stats.at[it, g, d], stat_send.at[it, g, d], stat_recv.at[it, g, d], cent_id(CENTS - d)
                )
            tops = [stats[it, g, d, 0:1, :] for d in range(CENTS)]
            top = tops[0]
            for other in tops[1:]:
                top = jnp.maximum(top, other)
            shares = [jnp.exp(other - top) for other in tops]
            total = shares[0] * stats[it, g, 0, 1:2, :]
            for d in range(1, CENTS):
                total = total + shares[d] * stats[it, g, d, 1:2, :]
            scale[0:1, g * GROUP : (g + 1) * GROUP] = shares[0] / total
            if it == 1:
                energy_out[0:1, g * GROUP : (g + 1) * GROUP] = top + jnp.log(total)

        for first in (True, False):
            start = ((1 - core) if first else core) * 256
            for g in range(GROUPS):
                if first:
                    merge(g)
                per = BLOCKS // GROUPS
                probs = jnp.concatenate(
                    [
                        (expo[j, rows(start, 256), :] * scale[0:1, j * BLOCK : (j + 1) * BLOCK]).astype(BF16)
                        for j in range(g * per, (g + 1) * per)
                    ],
                    axis=1,
                )
                term = jnp.dot(
                    probs, sample[g * GROUP : (g + 1) * GROUP, :], preferred_element_type=F32
                )
                if g:
                    sums[it, rows(start, 256), :] += term
                else:
                    sums[it, rows(start, 256), :] = term
            if first:
                send(
                    sums.at[it, rows(start, 256)], core32.at[it],
                    rs_send.at[1 + it, 0], rs_recv.at[1 + it, 0], sibling,
                )
        total = reduce_scatter(
            1 + it, OWN, sums.at[it], core32.at[it], x32.at[it], xs32.at[it], z32.at[it], zs32.at[it]
        )
        dst = centers.at[1] if it == 0 else centers_out
        dst[mine, :] = normalize(total).astype(BF16)
        all_gather(1 + it, dst)

    for copy in sent:
        copy.wait_send()


def on_device(embedding_pool, select_index, seed_index):
    vmem = pl.BlockSpec(memory_space=pltpu.VMEM)
    smem = pl.BlockSpec(memory_space=pltpu.SMEM)
    u = OWN * PARTS
    centers, energy = pl.pallas_call(
        kernel,
        out_shape=(
            jax.ShapeDtypeStruct((CENT, D), BF16),
            jax.ShapeDtypeStruct((1, ROWS), F32),
        ),
        in_specs=[pl.BlockSpec(memory_space=pl.ANY), smem, smem],
        out_specs=(vmem, vmem),
        scratch_shapes=[
            pltpu.VMEM((POOL, D), BF16),
            pltpu.VMEM(((POOL + 2) * PARTS, LANES), F32),
            pltpu.VMEM((ROWS * PARTS, LANES), F32),
            pltpu.VMEM((ROWS, D), BF16),
            pltpu.VMEM((CENT * PARTS, LANES), F32),
            pltpu.VMEM((BLOCKS, CENT, BLOCK), F32),
            pltpu.VMEM((2, CENT, BLOCK), F32),
            pltpu.VMEM((2, GROUPS, CENTS, 2, GROUP), F32),
            pltpu.VMEM((1, ROWS), F32),
            pltpu.VMEM((2, CENT, D), F32),
            pltpu.VMEM((CENT * PARTS, LANES), BF16),
            pltpu.VMEM((CENT * PARTS // 2, LANES), BF16),
            pltpu.VMEM((Z, u, LANES), BF16),
            pltpu.VMEM((Z, u, LANES), BF16),
            pltpu.VMEM((Z, u, LANES), BF16),
            pltpu.VMEM((Z, u, LANES), BF16),
            pltpu.VMEM((u, LANES), F32),
            pltpu.VMEM((2, CENT // 2, D), F32),
            pltpu.VMEM((2, Z, OWN, D), F32),
            pltpu.VMEM((2, Z, OWN, D), F32),
            pltpu.VMEM((2, Z, OWN, D), F32),
            pltpu.VMEM((2, Z, OWN, D), F32),
            pltpu.VMEM((2, CENT, D), BF16),
            pltpu.SemaphoreType.DMA((LOADS,)),
            pltpu.SemaphoreType.DMA((3, 16)),
            pltpu.SemaphoreType.DMA((3, 16)),
            pltpu.SemaphoreType.DMA((3, 32)),
            pltpu.SemaphoreType.DMA((3, 32)),
            pltpu.SemaphoreType.DMA((2, GROUPS, CENTS)),
            pltpu.SemaphoreType.DMA((2, GROUPS, CENTS)),
        ],
        compiler_params=pltpu.CompilerParams(
            collective_id=0, has_side_effects=True, vmem_limit_bytes=60 * 1024 * 1024
        ),
        cost_estimate=pl.CostEstimate(
            flops=8 * ROWS * CENT * D, bytes_accessed=POOL * D * 2, transcendentals=2 * ROWS * CENT
        ),
    )(embedding_pool, select_index, seed_index)
    return (centers, energy.reshape(ROWS))


def solution(mesh):
    placed = (P("row", None), P("row"), P("cent"))
    return jax.shard_map(
        on_device,
        mesh=mesh,
        in_specs=placed,
        out_specs=(P("cent", None), P("row")),
        check_vma=False,
    )
```

time: 1010 us -> 111 us (0.11)
  waiting for transfers between devices: 820 us -> 0 us
  Pallas kernels: 0 us -> 107 us
  blocking collectives: 100 us -> 0 us
  matrix products: 32.6 us -> 0 us
  local copies, waits for them, and re-layouts: 21.9 us -> 3.19 us
  other arithmetic: 17.3 us -> 0 us
  between operations: 13.8 us -> 0.64 us
    psum x3 -> x0, waiting for transfers between devices: 820 us -> none  [the longest x2 550 us: on_device(): sums = lax.psum(sums, 'row')]
    pallas_call x0 -> x1, Pallas kernels: none -> 107 us  [on_device(): pl.pallas_call(kernel, out_shape=(jax.ShapeDtypeStruct((CENT, D), BF16),...]
    pmax x2 -> x0, blocking collectives: 52.6 us -> none  [on_device(): top = lax.pmax(local_top, 'cent')]
    psum x2 -> x0, blocking collectives: 47.7 us -> none  [on_device(): total = lax.psum(jnp.sum(expo, axis=1), 'cent')]
    dot_general x5 -> x0, matrix products: 32.6 us -> none  [the longest x2 14.1 us: on_device(): lax.dot_general(probs, sample, (((0,), (0,)), ((), ())), preferred_elemen...]
    gather x1 -> x0, local copies, waits for them, and re-layouts: 21.9 us -> none  [on_device(): sample = jnp.take(embedding_pool, select_index, axis=0)]
    reduce_sum x5 -> x0, other arithmetic: 13 us -> none  [the longest x2 9.06 us: on_device(): total = lax.psum(jnp.sum(expo, axis=1), 'cent')]
  transfers between devices with their start and end apart: 3 -> 0, of which waited for: 3 -> 0; matrix products, arithmetic and copies ran while one was open for 0% -> 0% of each run, Pallas kernels for 0% -> 0%
where the time goes in v1:
time: 111 us
  Pallas kernels  107 us (96%)
  local copies, waits for them, and re-layouts  3.19 us (3%)
    pallas_call x1, Pallas kernels, on_device(): pl.pallas_call(kernel, out_shape=(jax.ShapeDtypeStruct((CENT, D), BF16),...  107 us
    unnamed x2, local copies, waits for them, and re-layouts  3.19 us

profile of v1, /device:TPU:1, one launch (start us, length us, event | category | flops | bytes accessed | tf_op | source)
XLA Modules:
  0.0 110.7 jit_solution(5529126527119227763)
XLA Ops:
  0.6 106.8 %shard_map.50 = (bf16[512,512]{1,0:T(8,128)(2,1)}, f32[1,4096]{1,0:T(1,128)}) custom-call(bf16[8192,512]{1,0:T(8,128)(2,1)} %pool_hbm.1, s32[4096]{0:T(1024)} %select.1, s32[512]{0:T(512)} %seed.1), custom_call_target="tpu_custom_call" | custom-call | flops 8589934592 | bytes 8388608 | tf_op jit(solution)/shard_map/pallas_call | solution.py:326
  107.5 1.9 %copy.7 = bf16[512,512]{1,0:T(8,128)(2,1)} copy(bf16[512,512]{1,0:T(8,128)(2,1)} %get-tuple-element.8) | data formatting | bytes 1048576
  109.3 1.3 %copy.8 = f32[4096]{0:T(1024)} copy(f32[4096]{0:T(1024)} %bitcast.1) | data formatting | bytes 32768

commit v2 on v1

v2 whole, which is shorter than its diff:
```python
import jax
import jax.numpy as jnp
from jax import lax
from jax.experimental import pallas as pl
from jax.experimental.pallas import tpu as pltpu
from jax.sharding import PartitionSpec as P

F32 = jnp.float32
BF16 = jnp.bfloat16
MESH = pl.DeviceIdType.MESH

POOL = 8192
ROWS = 4096
CENT = 512
HALF = CENT // 2
D = 512
LANES = 128
PARTS = D // LANES
LOADS = 16
BLOCK = 512
BLOCKS = ROWS // BLOCK
GROUPS = ((0, 2), (2, 4), (4, 7), (7, 8))
GROUP = 3 * BLOCK
OWN = 16
Z = 8
CENTS = 8
FAR_FIRST = (4, 3, 5, 2, 6, 1, 7)
NEAR_FIRST = FAR_FIRST[::-1]


def rows(start, size):
    return pl.ds(pl.multiple_of(start, size), size)


def normalize(v):
    return v * lax.rsqrt(jnp.sum(v * v, axis=1, keepdims=True) + 1e-06)


def pack(v):
    top = jnp.maximum(jnp.max(jnp.abs(v), axis=1, keepdims=True), 1e-30)
    exponent = jnp.ceil(jnp.log2(top))
    coded = jnp.round(v * (jnp.exp2(15.0 - exponent) * 0.999)).astype(jnp.int32)
    exponent = jnp.broadcast_to(exponent, (v.shape[0], LANES)).astype(jnp.int32)
    return jnp.concatenate([coded, exponent], axis=1).astype(jnp.int16)


def unpack(w):
    w = w.astype(jnp.int32).astype(F32)
    unit = jnp.exp2(w[:, D:] - 15.0) * (1.0 / 0.999)
    return jnp.concatenate([w[:, t * LANES : (t + 1) * LANES] * unit for t in range(PARTS)], axis=1)


def kernel(
    pool_hbm,
    select,
    seed,
    centers_out,
    energy_out,
    pool_in,
    pool32,
    sample32,
    sample,
    seeds32,
    expo,
    scores,
    local,
    stats,
    scale,
    sums,
    seeds16,
    core16,
    core32,
    own32,
    x_rx0,
    x_tx0,
    z_rx0,
    z_tx0,
    x_rx,
    x_tx,
    z_rx,
    z_tx,
    centers,
    load_sem,
    rs_send,
    rs_recv,
    ag_send,
    ag_recv,
    stat_send,
    stat_recv,
):
    row = lax.axis_index("row")
    cent = lax.axis_index("cent")
    xh = row // 16
    z = (row // 2) % Z
    core = row % 2

    def row_id(xh_, z_, core_):
        return xh_ * 16 + z_ * 2 + core_

    sibling = (row_id(xh, z, 1 - core), cent)
    across = (row_id(1 - xh, z, core), cent)

    def z_id(distance):
        return (row_id(xh, (z + distance) % Z, core), cent)

    def cent_id(distance):
        return (row, (cent + distance) % CENTS)

    sent = []

    def send(src, dst, send_sem, recv_sem, device):
        copy = pltpu.make_async_remote_copy(
            src_ref=src, dst_ref=dst, send_sem=send_sem, recv_sem=recv_sem,
            device_id=device, device_id_type=MESH,
        )
        copy.start()
        sent.append(copy)

    def drain():
        for copy in sent:
            copy.wait_send()
        sent.clear()

    def arrived(dst, send_sem, recv_sem, device):
        pltpu.make_async_remote_copy(
            src_ref=dst, dst_ref=dst, send_sem=send_sem, recv_sem=recv_sem,
            device_id=device, device_id_type=MESH,
        ).wait_recv()

    step = POOL // LOADS

    def load(i):
        part = rows(i * step, step)
        return pltpu.make_async_copy(pool_hbm.at[part], pool_in.at[part], load_sem.at[i])

    for i in range(LOADS):
        load(i).start()
    barrier = pltpu.get_barrier_semaphore()
    partners = [sibling, across] + [z_id(d) for d in range(1, Z)] + [cent_id(d) for d in range(1, CENTS)]
    for partner in partners:
        pl.semaphore_signal(barrier, inc=1, device_id=partner, device_id_type=MESH)

    def widen(i, carry):
        load(i).wait()
        for b in range(step // 128):
            start = pl.multiple_of(i * step + b * 128, 128)
            block = pool_in[pl.ds(start, 128), :].astype(F32)
            for t in range(PARTS):
                pool32[pl.ds(start * PARTS + t, 128, stride=PARTS), :] = block[:, t * LANES : (t + 1) * LANES]
        return carry

    lax.fori_loop(0, LOADS, widen, 0)
    pool32[POOL * PARTS :, :] = jnp.zeros((2 * PARTS, LANES), F32)

    def pick_seed(b, carry):
        for v in range(16):
            k = b * 16 + v
            where = seed[k]
            away = lax.shift_right_arithmetic(where, 12) - row
            away = jnp.minimum(jnp.maximum(away, -away), 1)
            index = select[jnp.bitwise_and(where, ROWS - 1)]
            index = index + (POOL - index) * away
            seeds32[pl.ds(pl.multiple_of(k * PARTS, PARTS), PARTS), :] = pool32[pl.ds(index * PARTS, PARTS), :]
        return carry

    lax.fori_loop(0, CENT // 16, pick_seed, 0)
    seeds16[...] = seeds32[...].astype(BF16)

    def gather(b, carry):
        for v in range(64):
            i = b * 64 + v
            index = select[i]
            sample32[pl.ds(pl.multiple_of(i * PARTS, PARTS), PARTS), :] = pool32[pl.ds(index * PARTS, PARTS), :]
        return carry

    def narrow(b, carry):
        start = b * 128
        for t in range(PARTS):
            sample[rows(start, 128), t * LANES : (t + 1) * LANES] = sample32[
                pl.ds(start * PARTS + t, 128, stride=PARTS), :
            ].astype(BF16)
        return carry

    def core_sems(phase, other):
        return rs_send.at[phase, 16 + other], rs_recv.at[phase, 16 + other]

    def reduce_scatter(phase, own, other, core_rx, x_rx, x_tx, z_rx, z_tx, code, decode, beside_x=None, beside_z=None):
        u = x_rx.shape[1]

        def sems(i):
            return rs_send.at[phase, i], rs_recv.at[phase, i]

        arrived(core_rx.at[1], *core_sems(phase, 1), sibling)
        for d in FAR_FIRST + (0,):
            w = (z + d) % Z
            x_tx[d] = code(other(w) + core_rx[1, rows(w * u, u), :].astype(F32))
            send(x_tx.at[d], x_rx.at[d], *sems(d), across)
        if beside_x:
            beside_x()
        arrived(core_rx.at[0], *core_sems(phase, 0), sibling)
        for d in FAR_FIRST + (0,):
            w = (z + d) % Z
            arrived(x_rx.at[d], *sems(d), across)
            total = (own(w) + core_rx[0, rows(w * u, u), :].astype(F32)) + decode(x_rx[d])
            if d:
                z_tx[d] = code(total)
                send(z_tx.at[d], z_rx.at[d], *sems(8 + d), z_id(d))
        if beside_z:
            beside_z()
        for d in NEAR_FIRST:
            arrived(z_rx.at[d], *sems(8 + d), z_id(Z - d))
            total = total + decode(z_rx[d])
        return total

    def part(dst, xh_, z_, core_):
        return dst.at[rows(xh_ * HALF + core_ * (Z * OWN) + z_ * OWN, OWN)]

    def ag_sems(phase, i):
        return ag_send.at[phase, i], ag_recv.at[phase, i]

    def gather_near(phase, dst, beside=None):
        mine = part(dst, xh, z, core)
        for d in FAR_FIRST:
            send(mine, mine, *ag_sems(phase, d), z_id(d))
        send(mine, mine, *ag_sems(phase, 8), across)
        send(mine, mine, *ag_sems(phase, 16), sibling)
        if beside:
            beside()
        for d in NEAR_FIRST:
            block = part(dst, xh, (z - d + Z) % Z, core)
            arrived(block, *ag_sems(phase, d), z_id(Z - d))
            send(block, block, *ag_sems(phase, 8 + d), across)
            send(block, block, *ag_sems(phase, 16 + d), sibling)
        for d in (0,) + NEAR_FIRST:
            arrived(part(dst, xh, (z - d + Z) % Z, 1 - core), *ag_sems(phase, 16 + d), sibling)

    def pass_on(phase, dst, i):
        d = ((0,) + NEAR_FIRST)[i]
        block = part(dst, 1 - xh, (z - d + Z) % Z, core)
        arrived(block, *ag_sems(phase, 8 + d), across)
        send(block, block, *ag_sems(phase, 24 + d), sibling)

    def gather_far(phase, dst):
        for d in (0,) + NEAR_FIRST:
            arrived(part(dst, 1 - xh, (z - d + Z) % Z, 1 - core), *ag_sems(phase, 24 + d), sibling)

    u = OWN * PARTS
    pl.semaphore_wait(barrier, len(partners))
    for other in (1, 0):
        side = (1 - xh) if other else xh
        send(
            seeds16.at[rows((side * 2 + 1 - core) * Z * u, Z * u)], core16.at[other],
            *core_sems(0, other), sibling,
        )

    def seeds_of(side):
        return lambda w: seeds16[rows((side * 2 + core) * Z * u + w * u, u), :].astype(F32)

    own32[...] = reduce_scatter(
        0, seeds_of(xh), seeds_of(1 - xh), core16, x_rx0, x_tx0, z_rx0, z_tx0,
        lambda v: v.astype(BF16), lambda v: v.astype(F32),
        lambda: lax.fori_loop(0, ROWS // 128, gather, 0),
        lambda: lax.fori_loop(ROWS // 128, ROWS // 64, gather, 0),
    )
    seeded = jnp.concatenate([own32[pl.ds(t, OWN, stride=PARTS), :] for t in range(PARTS)], axis=1)
    mine = rows(xh * HALF + core * (Z * OWN) + z * OWN, OWN)
    centers[0, mine, :] = normalize(seeded).astype(BF16)
    gather_near(0, centers.at[0], lambda: lax.fori_loop(0, ROWS // 128, narrow, 0))

    for it in range(2):
        current = centers.at[it]

        def stats_of(g, d):
            first, last = GROUPS[g]
            return stats.at[it, g, d, :, pl.ds(0, (last - first) * BLOCK)]

        def score(side, j):
            start = (xh if side == 0 else 1 - xh) * HALF
            scores[j % 2] = lax.dot_general(
                current[rows(start, HALF), :], sample[j * BLOCK : (j + 1) * BLOCK, :],
                (((1,), (1,)), ((), ())), preferred_element_type=F32,
            )

        def soften(side, j):
            slot = j % 2
            top = [scores[slot, 8 * i : 8 * i + 8, :] for i in range(2)]
            for i in range(2, HALF // 8):
                top[i % 2] = jnp.maximum(top[i % 2], scores[slot, 8 * i : 8 * i + 8, :])
            top = jnp.max(jnp.maximum(top[0], top[1]), axis=0, keepdims=True)
            total = [jnp.zeros((8, BLOCK), F32)] * 2
            for i in range(HALF // 8):
                e = jnp.exp(scores[slot, 8 * i : 8 * i + 8, :] - top)
                expo[side, j, 8 * i : 8 * i + 8, :] = e
                total[i % 2] = total[i % 2] + e
            total = jnp.sum(total[0] + total[1], axis=0, keepdims=True)
            columns = slice(j * BLOCK, (j + 1) * BLOCK)
            local[side, 0:1, columns] = top
            if side == 0:
                local[0, 1:2, columns] = total
            else:
                near = local[0, 0:1, columns]
                both = jnp.maximum(near, top)
                total = total * jnp.exp(top - both) + local[0, 1:2, columns] * jnp.exp(near - both)
                g = [first <= j < last for first, last in GROUPS].index(True)
                inside = slice((j - GROUPS[g][0]) * BLOCK, (j - GROUPS[g][0] + 1) * BLOCK)
                stats[it, g, 0, 0:1, inside] = both
                stats[it, g, 0, 1:2, inside] = total

        for side in (0, 1):
            if side:
                gather_far(it, current)
            score(side, 0)
            for j in range(BLOCKS):
                if j + 1 < BLOCKS:
                    score(side, j + 1)
                soften(side, j)
                if side == 0:
                    pass_on(it, current, j)
                elif j + 1 in [last for _, last in GROUPS]:
                    g = [last for _, last in GROUPS].index(j + 1)
                    for d in range(1, CENTS):
                        send(
                            stats_of(g, 0), stats_of(g, d),
                            stat_send.at[it, g, d], stat_recv.at[it, g, d], cent_id(d),
                        )

        def merge(g):
            for d in range(1, CENTS):
                arrived(
                    stats_of(g, d), stat_send.at[it, g, d], stat_recv.at[it, g, d], cent_id(CENTS - d)
                )
            first, last = GROUPS[g]
            size = (last - first) * BLOCK
            tops = [stats[it, g, d, 0:1, 0:size] for d in range(CENTS)]
            top = tops[0]
            for other in tops[1:]:
                top = jnp.maximum(top, other)
            total = jnp.exp(tops[0] - top) * stats[it, g, 0, 1:2, 0:size]
            for d in range(1, CENTS):
                total = total + jnp.exp(tops[d] - top) * stats[it, g, d, 1:2, 0:size]
            columns = slice(first * BLOCK, last * BLOCK)
            for side in range(2):
                scale[side, 0:1, columns] = jnp.exp(local[side, 0:1, columns] - top) / total
            if it == 1:
                energy_out[0:1, columns] = top + jnp.log(total)

        def add_up(side, g):
            probs = jnp.concatenate(
                [
                    (expo[side, j] * scale[side, 0:1, j * BLOCK : (j + 1) * BLOCK]).astype(BF16)
                    for j in range(*GROUPS[g])
                ],
                axis=1,
            )
            term = jnp.dot(probs, sample[GROUPS[g][0] * BLOCK : GROUPS[g][1] * BLOCK, :], preferred_element_type=F32)
            if g:
                sums[it, side] += term
            else:
                sums[it, side] = term

        def exchange(other):
            send(
                sums.at[it, other, rows((1 - core) * Z * OWN, Z * OWN)], core32.at[it, other],
                *core_sems(1 + it, other), sibling,
            )

        def sums_of(side):
            return lambda w: sums[it, side, rows(core * Z * OWN + w * OWN, OWN), :]

        for g in range(len(GROUPS)):
            merge(g)
            for side in (1, 0):
                add_up(side, g)
                if g == len(GROUPS) - 1:
                    exchange(side)
        total = reduce_scatter(
            1 + it, sums_of(0), sums_of(1), core32.at[it],
            x_rx.at[it], x_tx.at[it], z_rx.at[it], z_tx.at[it], pack, unpack, None, drain,
        )
        dst = centers.at[1] if it == 0 else centers_out
        dst[mine, :] = normalize(total).astype(BF16)
        gather_near(1 + it, dst)
    for i in range(Z):
        pass_on(2, centers_out, i)
    drain()
    gather_far(2, centers_out)


def hand_on(centers_in, energy_in, centers_out, energy_out):
    centers_out[...] = centers_in[...]
    energy_out[...] = energy_in[...]


def on_device(embedding_pool, select_index, seed_index):
    vmem = pl.BlockSpec(memory_space=pltpu.VMEM)
    smem = pl.BlockSpec(memory_space=pltpu.SMEM)
    u = OWN * PARTS
    seed_slots = pltpu.VMEM((Z, u, LANES), BF16)
    slots = pltpu.VMEM((2, Z, OWN, D + LANES), jnp.int16)
    centers, energy = pl.pallas_call(
        kernel,
        out_shape=(
            jax.ShapeDtypeStruct((CENT, D), BF16),
            jax.ShapeDtypeStruct((1, ROWS), F32),
        ),
        in_specs=[pl.BlockSpec(memory_space=pl.ANY), smem, smem],
        out_specs=(vmem, vmem),
        scratch_shapes=[
            pltpu.VMEM((POOL, D), BF16),
            pltpu.VMEM(((POOL + 2) * PARTS, LANES), F32),
            pltpu.VMEM((ROWS * PARTS, LANES), F32),
            pltpu.VMEM((ROWS, D), BF16),
            pltpu.VMEM((CENT * PARTS, LANES), F32),
            pltpu.VMEM((2, BLOCKS, HALF, BLOCK), F32),
            pltpu.VMEM((2, HALF, BLOCK), F32),
            pltpu.VMEM((2, 2, ROWS), F32),
            pltpu.VMEM((2, len(GROUPS), CENTS, 2, GROUP), F32),
            pltpu.VMEM((2, 1, ROWS), F32),
            pltpu.VMEM((2, 2, HALF, D), F32),
            pltpu.VMEM((CENT * PARTS, LANES), BF16),
            pltpu.VMEM((2, Z * u, LANES), BF16),
            pltpu.VMEM((2, 2, Z * OWN, D), F32),
            pltpu.VMEM((u, LANES), F32),
            seed_slots, seed_slots, seed_slots, seed_slots,
            slots, slots, slots, slots,
            pltpu.VMEM((2, CENT, D), BF16),
            pltpu.SemaphoreType.DMA((LOADS,)),
            pltpu.SemaphoreType.DMA((3, 18)),
            pltpu.SemaphoreType.DMA((3, 18)),
            pltpu.SemaphoreType.DMA((3, 32)),
            pltpu.SemaphoreType.DMA((3, 32)),
            pltpu.SemaphoreType.DMA((2, len(GROUPS), CENTS)),
            pltpu.SemaphoreType.DMA((2, len(GROUPS), CENTS)),
        ],
        compiler_params=pltpu.CompilerParams(
            collective_id=0, has_side_effects=True, vmem_limit_bytes=60 * 1024 * 1024
        ),
        cost_estimate=pl.CostEstimate(
            flops=8 * ROWS * CENT * D, bytes_accessed=POOL * D * 2, transcendentals=2 * ROWS * CENT
        ),
    )(embedding_pool, select_index, seed_index)
    return pl.pallas_call(
        hand_on,
        out_shape=(
            jax.ShapeDtypeStruct((CENT, D), BF16),
            jax.ShapeDtypeStruct((ROWS,), F32),
        ),
        in_specs=[vmem, vmem],
        out_specs=(vmem, vmem),
        cost_estimate=pl.CostEstimate(flops=0, bytes_accessed=4 * CENT * D + 8 * ROWS, transcendentals=0),
    )(centers, energy.reshape(ROWS))


def solution(mesh):
    placed = (P("row", None), P("row"), P("cent"))
    return jax.shard_map(
        on_device,
        mesh=mesh,
        in_specs=placed,
        out_specs=(P("cent", None), P("row")),
        check_vma=False,
    )
```

time: 111 us -> 101 us (0.910)
  Pallas kernels: 107 us -> 99.7 us
  local copies, waits for them, and re-layouts: 3.19 us -> 0 us
    pallas_call x1, Pallas kernels: 107 us -> 97.8 us  [on_device(): pl.pallas_call(kernel, out_shape=(jax.ShapeDtypeStruct((CENT, D), BF16),...]
    unnamed x2 -> x0, local copies, waits for them, and re-layouts: 3.19 us -> none
    pallas_call x0 -> x1, Pallas kernels: none -> 1.87 us  [on_device(): pl.pallas_call(hand_on, out_shape=(jax.ShapeDtypeStruct((CENT, D), BF16),...]
where the time goes in v2:
time: 101 us; the launch traced here: 100 us
  Pallas kernels  99.7 us (99%)
    pallas_call x1, Pallas kernels, on_device(): pl.pallas_call(kernel, out_shape=(jax.ShapeDtypeStruct((CENT, D), BF16),...  97.8 us

profile of v2, /device:TPU:1, one launch (start us, length us, event | category | flops | bytes accessed | tf_op | source)
XLA Modules:
  0.0 100.3 jit_solution(11391555528326077059)
XLA Ops:
  0.6 97.8 %shard_map.50 = (bf16[512,512]{1,0:T(8,128)(2,1)}, f32[1,4096]{1,0:T(1,128)}) custom-call(bf16[8192,512]{1,0:T(8,128)(2,1)} %pool_hbm.1, s32[4096]{0:T(1024)} %select.1, s32[512]{0:T(512)} %seed.1), custom_call_target="tpu_custom_call" | custom-call | flops 8589934592 | bytes 8388608 | tf_op jit(solution)/shard_map/pallas_call | solution.py:400
  98.5 1.9 %shard_map.51 = (bf16[512,512]{1,0:T(8,128)(2,1)}, f32[4096]{0:T(1024)}) custom-call(bf16[512,512]{1,0:T(8,128)(2,1)} %get-tuple-element.4.centers_in, f32[4096]{0:T(1024)} %bitcast.1), custom_call_target="tpu_custom_call" | custom-call | bytes 1081344 | tf_op jit(solution)/shard_map/pallas_call | solution.py:442

commit v3 on v2

--- a/solution.py
+++ b/solution.py
@@ -12,15 +12,18 @@
 POOL = 8192
 ROWS = 4096
 CENT = 512
-HALF = CENT // 2
+CHIP_ROWS = 2 * ROWS
+HALF = CENT // 4
 D = 512
 LANES = 128
 PARTS = D // LANES
 LOADS = 16
-BLOCK = 512
-BLOCKS = ROWS // BLOCK
+BLOCK = 1024
+BLOCKS = CHIP_ROWS // BLOCK
+PIECE = 1024
 GROUPS = ((0, 2), (2, 4), (4, 7), (7, 8))
 GROUP = 3 * BLOCK
+JOINS = {4: (0,), 6: (1,), 7: (2, 3)}
 OWN = 16
 Z = 8
 CENTS = 8
@@ -30,6 +33,16 @@
 
 def rows(start, size):
     return pl.ds(pl.multiple_of(start, size), size)
+
+
+def log_sum(logs):
+    top = logs[0]
+    for other in logs[1:]:
+        top = jnp.maximum(top, other)
+    total = jnp.exp(logs[0] - top)
+    for other in logs[1:]:
+        total = total + jnp.exp(other - top)
+    return top + jnp.log(total)
 
 
 def normalize(v):
@@ -64,12 +77,13 @@
     expo,
     scores,
     local,
+    pair,
     stats,
     scale,
     sums,
     seeds16,
     core16,
-    core32,
+    energy,
     own32,
     x_rx0,
     x_tx0,
@@ -87,6 +101,10 @@
     ag_recv,
     stat_send,
     stat_recv,
+    pair_send,
+    pair_recv,
+    sample_send,
+    sample_recv,
 ):
     row = lax.axis_index("row")
     cent = lax.axis_index("cent")
@@ -166,42 +184,56 @@
     lax.fori_loop(0, CENT // 16, pick_seed, 0)
     seeds16[...] = seeds32[...].astype(BF16)
 
-    def gather(b, carry):
-        for v in range(64):
-            i = b * 64 + v
-            index = select[i]
-            sample32[pl.ds(pl.multiple_of(i * PARTS, PARTS), PARTS), :] = pool32[pl.ds(index * PARTS, PARTS), :]
-        return carry
-
-    def narrow(b, carry):
-        start = b * 128
-        for t in range(PARTS):
-            sample[rows(start, 128), t * LANES : (t + 1) * LANES] = sample32[
-                pl.ds(start * PARTS + t, 128, stride=PARTS), :
-            ].astype(BF16)
-        return carry
+    def gather_piece(p):
+        def gather(b, carry):
+            for v in range(64):
+                i = b * 64 + v
+                index = select[p * PIECE + i]
+                sample32[pl.ds(pl.multiple_of(i * PARTS, PARTS), PARTS), :] = pool32[
+                    pl.ds(index * PARTS, PARTS), :
+                ]
+            return carry
+
+        def narrow(b, carry):
+            start = b * 128
+            for t in range(PARTS):
+                sample[rows(core * ROWS + p * PIECE + start, 128), t * LANES : (t + 1) * LANES] = sample32[
+                    pl.ds(start * PARTS + t, 128, stride=PARTS), :
+                ].astype(BF16)
+            return carry
+
+        lax.fori_loop(0, PIECE // 64, gather, 0)
+        lax.fori_loop(0, PIECE // 128, narrow, 0)
+
+    def gather_pieces(first, last):
+        for p in range(first, last):
+            gather_piece(p)
+
+    def share_samples():
+        for p in range(ROWS // PIECE):
+            piece = sample.at[rows(core * ROWS + p * PIECE, PIECE)]
+            send(piece, piece, sample_send.at[p], sample_recv.at[p], sibling)
+
+    def beside_z():
+        gather_pieces(2, 4)
+        share_samples()
 
     def core_sems(phase, other):
         return rs_send.at[phase, 16 + other], rs_recv.at[phase, 16 + other]
 
-    def reduce_scatter(phase, own, other, core_rx, x_rx, x_tx, z_rx, z_tx, code, decode, beside_x=None, beside_z=None):
-        u = x_rx.shape[1]
-
+    def reduce_scatter(phase, own, other, x_rx, x_tx, z_rx, z_tx, code, decode, beside_x=None, beside_z=None):
         def sems(i):
             return rs_send.at[phase, i], rs_recv.at[phase, i]
 
-        arrived(core_rx.at[1], *core_sems(phase, 1), sibling)
+        u = x_rx.shape[1]
+        x_tx[...] = code(other)
         for d in FAR_FIRST + (0,):
-            w = (z + d) % Z
-            x_tx[d] = code(other(w) + core_rx[1, rows(w * u, u), :].astype(F32))
-            send(x_tx.at[d], x_rx.at[d], *sems(d), across)
+            send(x_tx.at[rows((z + d) % Z * u, u)], x_rx.at[d], *sems(d), across)
         if beside_x:
             beside_x()
-        arrived(core_rx.at[0], *core_sems(phase, 0), sibling)
         for d in FAR_FIRST + (0,):
-            w = (z + d) % Z
             arrived(x_rx.at[d], *sems(d), across)
-            total = (own(w) + core_rx[0, rows(w * u, u), :].astype(F32)) + decode(x_rx[d])
+            total = own((z + d) % Z) + decode(x_rx[d])
             if d:
                 z_tx[d] = code(total)
                 send(z_tx.at[d], z_rx.at[d], *sems(8 + d), z_id(d))
@@ -213,10 +245,27 @@
         return total
 
     def part(dst, xh_, z_, core_):
-        return dst.at[rows(xh_ * HALF + core_ * (Z * OWN) + z_ * OWN, OWN)]
+        return dst.at[rows(xh_ * (2 * HALF) + core_ * HALF + z_ * OWN, OWN)]
 
     def ag_sems(phase, i):
         return ag_send.at[phase, i], ag_recv.at[phase, i]
+
+    def scored(dst, side, d):
+        return dst.at[rows(side * HALF + (z - d + Z) % Z * OWN, OWN)]
+
+    def spread_near(phase, dst):
+        mine = scored(dst, 0, 0)
+        for d in FAR_FIRST:
+            send(mine, mine, *ag_sems(phase, d), z_id(d))
+        send(mine, scored(dst, 1, 0), *ag_sems(phase, 8), across)
+        for d in NEAR_FIRST:
+            block = scored(dst, 0, d)
+            arrived(block, *ag_sems(phase, d), z_id(Z - d))
+            send(block, scored(dst, 1, d), *ag_sems(phase, 8 + d), across)
+
+    def spread_far(phase, dst):
+        for d in (0,) + NEAR_FIRST:
+            arrived(scored(dst, 1, d), *ag_sems(phase, 8 + d), across)
 
     def gather_near(phase, dst, beside=None):
         mine = part(dst, xh, z, core)
@@ -253,19 +302,30 @@
             *core_sems(0, other), sibling,
         )
 
-    def seeds_of(side):
-        return lambda w: seeds16[rows((side * 2 + core) * Z * u + w * u, u), :].astype(F32)
+    arrived(core16.at[1], *core_sems(0, 1), sibling)
+
+    def beside_x():
+        gather_pieces(0, 2)
+        arrived(core16.at[0], *core_sems(0, 0), sibling)
+
+    def own_seeds(w):
+        return (seeds16[rows((xh * 2 + core) * Z * u + w * u, u), :].astype(F32)
+                + core16[0, rows(w * u, u), :].astype(F32))
+
+    other_seeds = seeds16[rows(((1 - xh) * 2 + core) * Z * u, Z * u), :].astype(F32) + core16[1].astype(F32)
 
     own32[...] = reduce_scatter(
-        0, seeds_of(xh), seeds_of(1 - xh), core16, x_rx0, x_tx0, z_rx0, z_tx0,
+        0, own_seeds, other_seeds, x_rx0, x_tx0, z_rx0, z_tx0,
         lambda v: v.astype(BF16), lambda v: v.astype(F32),
-        lambda: lax.fori_loop(0, ROWS // 128, gather, 0),
-        lambda: lax.fori_loop(ROWS // 128, ROWS // 64, gather, 0),
+        beside_x, beside_z,
     )
     seeded = jnp.concatenate([own32[pl.ds(t, OWN, stride=PARTS), :] for t in range(PARTS)], axis=1)
-    mine = rows(xh * HALF + core * (Z * OWN) + z * OWN, OWN)
-    centers[0, mine, :] = normalize(seeded).astype(BF16)
-    gather_near(0, centers.at[0], lambda: lax.fori_loop(0, ROWS // 128, narrow, 0))
+    centers[0, rows(z * OWN, OWN), :] = normalize(seeded).astype(BF16)
+    spread_near(0, centers.at[0])
+    for p in range(ROWS // PIECE):
+        arrived(
+            sample.at[rows((1 - core) * ROWS + p * PIECE, PIECE)], sample_send.at[p], sample_recv.at[p], sibling
+        )
 
     for it in range(2):
         current = centers.at[it]
@@ -275,9 +335,8 @@
             return stats.at[it, g, d, :, pl.ds(0, (last - first) * BLOCK)]
 
         def score(side, j):
-            start = (xh if side == 0 else 1 - xh) * HALF
             scores[j % 2] = lax.dot_general(
-                current[rows(start, HALF), :], sample[j * BLOCK : (j + 1) * BLOCK, :],
+                current[side * HALF : (side + 1) * HALF, :], sample[j * BLOCK : (j + 1) * BLOCK, :],
                 (((1,), (1,)), ((), ())), preferred_element_type=F32,
             )
 
@@ -290,7 +349,7 @@
             total = [jnp.zeros((8, BLOCK), F32)] * 2
             for i in range(HALF // 8):
                 e = jnp.exp(scores[slot, 8 * i : 8 * i + 8, :] - top)
-                expo[side, j, 8 * i : 8 * i + 8, :] = e
+                expo[j, side * HALF + 8 * i : side * HALF + 8 * i + 8, :] = e
                 total[i % 2] = total[i % 2] + e
             total = jnp.sum(total[0] + total[1], axis=0, keepdims=True)
             columns = slice(j * BLOCK, (j + 1) * BLOCK)
@@ -303,26 +362,33 @@
                 total = total * jnp.exp(top - both) + local[0, 1:2, columns] * jnp.exp(near - both)
                 g = [first <= j < last for first, last in GROUPS].index(True)
                 inside = slice((j - GROUPS[g][0]) * BLOCK, (j - GROUPS[g][0] + 1) * BLOCK)
-                stats[it, g, 0, 0:1, inside] = both
-                stats[it, g, 0, 1:2, inside] = total
+                pair[it, g, 0, 0:1, inside] = both + jnp.log(total)
+
+        def pair_of(g, c):
+            first, last = GROUPS[g]
+            return pair.at[it, g, c, :, pl.ds(0, (last - first) * BLOCK)]
+
+        def join(g):
+            arrived(pair_of(g, 1), pair_send.at[it, g], pair_recv.at[it, g], sibling)
+            inside = slice(0, (GROUPS[g][1] - GROUPS[g][0]) * BLOCK)
+            stats[it, g, 0, 0:1, inside] = log_sum([pair[it, g, c, 0:1, inside] for c in range(2)])
+            for d in range(1, CENTS):
+                send(stats_of(g, 0), stats_of(g, d), stat_send.at[it, g, d], stat_recv.at[it, g, d], cent_id(d))
 
         for side in (0, 1):
             if side:
-                gather_far(it, current)
+                spread_far(it, current)
             score(side, 0)
             for j in range(BLOCKS):
                 if j + 1 < BLOCKS:
                     score(side, j + 1)
                 soften(side, j)
-                if side == 0:
-                    pass_on(it, current, j)
-                elif j + 1 in [last for _, last in GROUPS]:
+                if side and j + 1 in [last for _, last in GROUPS]:
                     g = [last for _, last in GROUPS].index(j + 1)
-                    for d in range(1, CENTS):
-                        send(
-                            stats_of(g, 0), stats_of(g, d),
-                            stat_send.at[it, g, d], stat_recv.at[it, g, d], cent_id(d),
-                        )
+                    send(pair_of(g, 0), pair_of(g, 1), pair_send.at[it, g], pair_recv.at[it, g], sibling)
+                if side:
+                    for g in JOINS.get(j, ()):
+                        join(g)
 
         def merge(g):
             for d in range(1, CENTS):
@@ -331,55 +397,53 @@
                 )
             first, last = GROUPS[g]
             size = (last - first) * BLOCK
-            tops = [stats[it, g, d, 0:1, 0:size] for d in range(CENTS)]
-            top = tops[0]
-            for other in tops[1:]:
-                top = jnp.maximum(top, other)
-            total = jnp.exp(tops[0] - top) * stats[it, g, 0, 1:2, 0:size]
-            for d in range(1, CENTS):
-                total = total + jnp.exp(tops[d] - top) * stats[it, g, d, 1:2, 0:size]
+            total = log_sum([stats[it, g, d, 0:1, 0:size] for d in range(CENTS)])
             columns = slice(first * BLOCK, last * BLOCK)
             for side in range(2):
-                scale[side, 0:1, columns] = jnp.exp(local[side, 0:1, columns] - top) / total
+                scale[side, 0:1, columns] = jnp.exp(local[side, 0:1, columns] - total)
             if it == 1:
-                energy_out[0:1, columns] = top + jnp.log(total)
-
-        def add_up(side, g):
+                energy[0:1, columns] = total
+
+        def add_up(g):
             probs = jnp.concatenate(
                 [
-                    (expo[side, j] * scale[side, 0:1, j * BLOCK : (j + 1) * BLOCK]).astype(BF16)
+                    jnp.concatenate(
+                        [
+                            (expo[j, side * HALF : (side + 1) * HALF, :]
+                             * scale[side, 0:1, j * BLOCK : (j + 1) * BLOCK]).astype(BF16)
+                            for side in range(2)
+                        ],
+                        axis=0,
+                    )
                     for j in range(*GROUPS[g])
                 ],
                 axis=1,
             )
-            term = jnp.dot(probs, sample[GROUPS[g][0] * BLOCK : GROUPS[g][1] * BLOCK, :], preferred_element_type=F32)
+            term = jnp.dot(
+                probs, sample[GROUPS[g][0] * BLOCK : GROUPS[g][1] * BLOCK, :], preferred_element_type=F32
+            )
             if g:
-                sums[it, side] += term
+                sums[it] += term
             else:
-                sums[it, side] = term
-
-        def exchange(other):
-            send(
-                sums.at[it, other, rows((1 - core) * Z * OWN, Z * OWN)], core32.at[it, other],
-                *core_sems(1 + it, other), sibling,
-            )
-
-        def sums_of(side):
-            return lambda w: sums[it, side, rows(core * Z * OWN + w * OWN, OWN), :]
+                sums[it] = term
+
+        def own_sums(w):
+            return sums[it, rows(w * OWN, OWN), :]
 
         for g in range(len(GROUPS)):
             merge(g)
-            for side in (1, 0):
-                add_up(side, g)
-                if g == len(GROUPS) - 1:
-                    exchange(side)
+            add_up(g)
         total = reduce_scatter(
-            1 + it, sums_of(0), sums_of(1), core32.at[it],
+            1 + it, own_sums, sums[it, HALF:, :],
             x_rx.at[it], x_tx.at[it], z_rx.at[it], z_tx.at[it], pack, unpack, None, drain,
         )
-        dst = centers.at[1] if it == 0 else centers_out
-        dst[mine, :] = normalize(total).astype(BF16)
-        gather_near(1 + it, dst)
+        if it == 0:
+            centers[1, rows(z * OWN, OWN), :] = normalize(total).astype(BF16)
+            spread_near(1, centers.at[1])
+    mine = rows(xh * (2 * HALF) + core * HALF + z * OWN, OWN)
+    centers_out[mine, :] = normalize(total).astype(BF16)
+    energy_out[...] = energy[:, rows(core * ROWS, ROWS)]
+    gather_near(2, centers_out)
     for i in range(Z):
         pass_on(2, centers_out, i)
     drain()
@@ -408,22 +472,29 @@
         scratch_shapes=[
             pltpu.VMEM((POOL, D), BF16),
             pltpu.VMEM(((POOL + 2) * PARTS, LANES), F32),
-            pltpu.VMEM((ROWS * PARTS, LANES), F32),
-            pltpu.VMEM((ROWS, D), BF16),
+            pltpu.VMEM((PIECE * PARTS, LANES), F32),
+            pltpu.VMEM((CHIP_ROWS, D), BF16),
             pltpu.VMEM((CENT * PARTS, LANES), F32),
-            pltpu.VMEM((2, BLOCKS, HALF, BLOCK), F32),
+            pltpu.VMEM((BLOCKS, 2 * HALF, BLOCK), F32),
             pltpu.VMEM((2, HALF, BLOCK), F32),
-            pltpu.VMEM((2, 2, ROWS), F32),
-            pltpu.VMEM((2, len(GROUPS), CENTS, 2, GROUP), F32),
-            pltpu.VMEM((2, 1, ROWS), F32),
-            pltpu.VMEM((2, 2, HALF, D), F32),
+            pltpu.VMEM((2, 2, CHIP_ROWS), F32),
+            pltpu.VMEM((2, len(GROUPS), 2, 1, GROUP), F32),
+            pltpu.VMEM((2, len(GROUPS), CENTS, 1, GROUP), F32),
+            pltpu.VMEM((2, 1, CHIP_ROWS), F32),
+            pltpu.VMEM((2, 2 * HALF, D), F32),
             pltpu.VMEM((CENT * PARTS, LANES), BF16),
             pltpu.VMEM((2, Z * u, LANES), BF16),
-            pltpu.VMEM((2, 2, Z * OWN, D), F32),
+            pltpu.VMEM((1, CHIP_ROWS), F32),
             pltpu.VMEM((u, LANES), F32),
-            seed_slots, seed_slots, seed_slots, seed_slots,
-            slots, slots, slots, slots,
-            pltpu.VMEM((2, CENT, D), BF16),
+            seed_slots,
+            pltpu.VMEM((Z * u, LANES), BF16),
+            seed_slots,
+            seed_slots,
+            slots,
+            pltpu.VMEM((2, Z * OWN, D + LANES), jnp.int16),
+            slots,
+            slots,
+            pltpu.VMEM((2, 2 * HALF, D), BF16),
             pltpu.SemaphoreType.DMA((LOADS,)),
             pltpu.SemaphoreType.DMA((3, 18)),
             pltpu.SemaphoreType.DMA((3, 18)),
@@ -431,6 +502,10 @@
             pltpu.SemaphoreType.DMA((3, 32)),
             pltpu.SemaphoreType.DMA((2, len(GROUPS), CENTS)),
             pltpu.SemaphoreType.DMA((2, len(GROUPS), CENTS)),
+            pltpu.SemaphoreType.DMA((2, len(GROUPS))),
+            pltpu.SemaphoreType.DMA((2, len(GROUPS))),
+            pltpu.SemaphoreType.DMA((ROWS // PIECE,)),
+            pltpu.SemaphoreType.DMA((ROWS // PIECE,)),
         ],
         compiler_params=pltpu.CompilerParams(
             collective_id=0, has_side_effects=True, vmem_limit_bytes=60 * 1024 * 1024

time: 101 us -> 98.1 us (0.971)
  Pallas kernels: 99.7 us -> 97.3 us
    pallas_call x1, Pallas kernels: 97.8 us -> 95.4 us  [on_device(): pl.pallas_call(kernel, out_shape=(jax.ShapeDtypeStruct((CENT, D), BF16),...]
where the time goes in v3:
time: 98.1 us; the launch traced here: 97.9 us
  Pallas kernels  97.3 us (99%)
    pallas_call x1, Pallas kernels, on_device(): pl.pallas_call(kernel, out_shape=(jax.ShapeDtypeStruct((CENT, D), BF16),...  95.4 us

profile of v3, /device:TPU:1, one launch (start us, length us, event | category | flops | bytes accessed | tf_op | source)
XLA Modules:
  0.0 97.9 jit_solution(17513432890903914644)
XLA Ops:
  0.6 95.4 %shard_map.50 = (bf16[512,512]{1,0:T(8,128)(2,1)}, f32[1,4096]{1,0:T(1,128)}) custom-call(bf16[8192,512]{1,0:T(8,128)(2,1)} %pool_hbm.1, s32[4096]{0:T(1024)} %select.1, s32[512]{0:T(512)} %seed.1), custom_call_target="tpu_custom_call" | custom-call | flops 8589934592 | bytes 8388608 | tf_op jit(solution)/shard_map/pallas_call | solution.py:464
  96.1 1.9 %shard_map.51 = (bf16[512,512]{1,0:T(8,128)(2,1)}, f32[4096]{0:T(1024)}) custom-call(bf16[512,512]{1,0:T(8,128)(2,1)} %get-tuple-element.4.centers_in, f32[4096]{0:T(1024)} %bitcast.1), custom_call_target="tpu_custom_call" | custom-call | bytes 1081344 | tf_op jit(solution)/shard_map/pallas_call | solution.py:517

commit v4 on v3

--- a/solution.py
+++ b/solution.py
@@ -65,10 +65,12 @@
 
 def kernel(
     pool_hbm,
+    select_hbm,
+    seed_hbm,
+    centers_out,
+    energy_out,
     select,
     seed,
-    centers_out,
-    energy_out,
     pool_in,
     pool32,
     sample32,
@@ -95,6 +97,7 @@
     z_tx,
     centers,
     load_sem,
+    index_sem,
     rs_send,
     rs_recv,
     ag_send,
@@ -151,12 +154,20 @@
         part = rows(i * step, step)
         return pltpu.make_async_copy(pool_hbm.at[part], pool_in.at[part], load_sem.at[i])
 
-    for i in range(LOADS):
+    for i in range(LOADS // 4):
         load(i).start()
+    indices = [
+        pltpu.make_async_copy(select_hbm, select, index_sem.at[0]),
+        pltpu.make_async_copy(seed_hbm, seed, index_sem.at[1]),
+    ]
+    for copy in indices:
+        copy.start()
     barrier = pltpu.get_barrier_semaphore()
-    partners = [sibling, across] + [z_id(d) for d in range(1, Z)] + [cent_id(d) for d in range(1, CENTS)]
+    partners = [z_id(d) for d in FAR_FIRST] + [cent_id(d) for d in range(1, CENTS)] + [across, sibling]
     for partner in partners:
         pl.semaphore_signal(barrier, inc=1, device_id=partner, device_id_type=MESH)
+    for i in range(LOADS // 4, LOADS):
+        load(i).start()
 
     def widen(i, carry):
         load(i).wait()
@@ -168,6 +179,8 @@
         return carry
 
     lax.fori_loop(0, LOADS, widen, 0)
+    for copy in indices:
+        copy.wait()
     pool32[POOL * PARTS :, :] = jnp.zeros((2 * PARTS, LANES), F32)
 
     def pick_seed(b, carry):
@@ -404,14 +417,15 @@
             if it == 1:
                 energy[0:1, columns] = total
 
-        def add_up(g):
+        def add_up(g, sides):
+            part = pl.ds(sides[0] * HALF, len(sides) * HALF)
             probs = jnp.concatenate(
                 [
                     jnp.concatenate(
                         [
                             (expo[j, side * HALF : (side + 1) * HALF, :]
                              * scale[side, 0:1, j * BLOCK : (j + 1) * BLOCK]).astype(BF16)
-                            for side in range(2)
+                            for side in sides
                         ],
                         axis=0,
                     )
@@ -423,19 +437,22 @@
                 probs, sample[GROUPS[g][0] * BLOCK : GROUPS[g][1] * BLOCK, :], preferred_element_type=F32
             )
             if g:
-                sums[it] += term
+                sums[it, part, :] += term
             else:
-                sums[it] = term
+                sums[it, part, :] = term
 
         def own_sums(w):
             return sums[it, rows(w * OWN, OWN), :]
 
-        for g in range(len(GROUPS)):
+        final = len(GROUPS) - 1
+        for g in range(final):
             merge(g)
-            add_up(g)
+            add_up(g, (0, 1))
+        merge(final)
+        add_up(final, (1,))
         total = reduce_scatter(
             1 + it, own_sums, sums[it, HALF:, :],
-            x_rx.at[it], x_tx.at[it], z_rx.at[it], z_tx.at[it], pack, unpack, None, drain,
+            x_rx.at[it], x_tx.at[it], z_rx.at[it], z_tx.at[it], pack, unpack, lambda: add_up(final, (0,)), drain,
         )
         if it == 0:
             centers[1, rows(z * OWN, OWN), :] = normalize(total).astype(BF16)
@@ -457,7 +474,6 @@
 
 def on_device(embedding_pool, select_index, seed_index):
     vmem = pl.BlockSpec(memory_space=pltpu.VMEM)
-    smem = pl.BlockSpec(memory_space=pltpu.SMEM)
     u = OWN * PARTS
     seed_slots = pltpu.VMEM((Z, u, LANES), BF16)
     slots = pltpu.VMEM((2, Z, OWN, D + LANES), jnp.int16)
@@ -467,9 +483,11 @@
             jax.ShapeDtypeStruct((CENT, D), BF16),
             jax.ShapeDtypeStruct((1, ROWS), F32),
         ),
-        in_specs=[pl.BlockSpec(memory_space=pl.ANY), smem, smem],
+        in_specs=[pl.BlockSpec(memory_space=pl.ANY)] * 3,
         out_specs=(vmem, vmem),
         scratch_shapes=[
+            pltpu.SMEM((ROWS,), jnp.int32),
+            pltpu.SMEM((CENT,), jnp.int32),
             pltpu.VMEM((POOL, D), BF16),
             pltpu.VMEM(((POOL + 2) * PARTS, LANES), F32),
             pltpu.VMEM((PIECE * PARTS, LANES), F32),
@@ -496,6 +514,7 @@
             slots,
             pltpu.VMEM((2, 2 * HALF, D), BF16),
             pltpu.SemaphoreType.DMA((LOADS,)),
+            pltpu.SemaphoreType.DMA((2,)),
             pltpu.SemaphoreType.DMA((3, 18)),
             pltpu.SemaphoreType.DMA((3, 18)),
             pltpu.SemaphoreType.DMA((3, 32)),

time: 98.1 us -> 97.8 us (level)
  no operation moved by 1% of the time
where the time goes in v4:
time: 97.8 us; the launch traced here: 97.7 us
  Pallas kernels  97 us (99%)
    pallas_call x1, Pallas kernels, on_device(): pl.pallas_call(kernel, out_shape=(jax.ShapeDtypeStruct((CENT, D), BF16),...  95.1 us

profile of v4, /device:TPU:1, one launch (start us, length us, event | category | flops | bytes accessed | tf_op | source)
XLA Modules:
  0.0 97.7 jit_solution(11788309759625022183)
XLA Ops:
  0.6 95.1 %shard_map.50 = (bf16[512,512]{1,0:T(8,128)(2,1)}, f32[1,4096]{1,0:T(1,128)}) custom-call(bf16[8192,512]{1,0:T(8,128)(2,1)} %pool_hbm.1, s32[4096]{0:T(1024)} %select_hbm.1, s32[512]{0:T(512)} %seed_hbm.1), custom_call_target="tpu_custom_call" | custom-call | flops 8589934592 | bytes 8388608 | tf_op jit(solution)/shard_map/pallas_call | solution.py:480
  95.8 1.9 %shard_map.51 = (bf16[512,512]{1,0:T(8,128)(2,1)}, f32[4096]{0:T(1024)}) custom-call(bf16[512,512]{1,0:T(8,128)(2,1)} %get-tuple-element.4.centers_in, f32[4096]{0:T(1024)} %bitcast.1), custom_call_target="tpu_custom_call" | custom-call | bytes 1081344 | tf_op jit(solution)/shard_map/pallas_call | solution.py:536
